TPU v7x, 32 devices: a whole 2x2x4 slice. The times are simulated.
32 devices in a mesh: seq: 8 (over z, y), tp: 4 (over x, core).
Axes of the slice: x: 2, y: 2, z: 4, core: 2. Of those that a mesh axis runs over, the one named last changes fastest.
Arguments:
- stream_in: bfloat16 [1024, 2880], P('seq'), may hold values from -40 to 40
- attn_gain: float32 [2880], replicated, may hold values from 0.1 to 1.9
- w_qkv: bfloat16 [2880, 8, 640], P(None, 'tp'), may hold values from -2 to 2
- key_value_cache: bfloat16 [128, 8, 128], P(None, 'tp'), may hold values from -6 to 6
- w_out: bfloat16 [4096, 2880], P('tp'), may hold values from -0.09375 to 0.09375
- mlp_gain: float32 [2880], replicated, may hold values from 0.1 to 1.9
- expert_index: int32 [1024, 4], P(('seq', 'tp')), may hold values from 0 to 31, all different within a row; in each aligned block of 32 rows (0 to 31, 32 to 63, ...) at most 8 rows name the same one
- gate_weight: float32 [1024, 4], P(('seq', 'tp')), may hold values from 0.05 to 0.5
- w_gateup: bfloat16 [32, 2880, 2, 2880], P('seq', None, None, 'tp'), may hold values from -0.109375 to 0.109375
- w_down: bfloat16 [32, 2880, 2880], P('seq', 'tp'), may hold values from -0.109375 to 0.109375
Outputs:
- stream_out: bfloat16 [1024, 2880], P(('seq', 'tp'))
Inputs may be any that keep to these rules, and one draw needn't show every extreme that they name: `expert_index`: in the rows of one device (aligned blocks of 32 rows) no expert is named by more than 8 rows, a bound that some block reaches; a row names 4 different experts.
All inputs are finite; a program needn't handle non-finite values.
Results may differ from a plain program's by a relative error of at most 0.01.
Values may be sent and summed in bfloat16 or wider, within the bound.
No kernel may reach another device: no remote copies, remote signals or barrier semaphores. Data moves between devices by JAX's collectives and lax.ppermute only.
A program may use at most 128 MiB of HBM per device.

v0:
```python
import jax
import jax.numpy as jnp
from jax import lax
from jax.sharding import PartitionSpec as P

MODEL_WIDTH = 2880
QUERY_HEADS = 64
KEY_VALUE_HEADS = 8
HEAD_SIZE = 64
WINDOW_KEYS = 128
EXPERTS = 32
TOPK = 4


EPS = 1e-05


def from_behind(value, axis, steps):
    count = lax.axis_size(axis)
    first, last = (max(0, -steps), min(count, count - steps))
    return lax.ppermute(value, axis, [(source, source + steps) for source in range(first, last)])


def rms_scale(values, gain_vec):
    mean_sq = jnp.mean(values * values, axis=-1, keepdims=True)
    return values * lax.rsqrt(mean_sq + EPS) * gain_vec


def window_block(queries, key_rows, value_rows):
    scores = jnp.einsum(
        "qhgc,khc->hgqk", queries, key_rows, preferred_element_type=jnp.float32
    ) * HEAD_SIZE ** (-0.5)
    key_offset = jnp.arange(key_rows.shape[0])[None, :] - jnp.arange(queries.shape[0])[:, None]
    in_window = (key_offset >= 1) & (key_offset <= WINDOW_KEYS)
    scores = jnp.where(in_window, scores, -1e30)
    row_max = jnp.max(scores, axis=-1, keepdims=True)
    exponent = jnp.exp(scores - row_max)
    layer_weights = (exponent / jnp.sum(exponent, axis=-1, keepdims=True)).astype(jnp.bfloat16)
    attended = jnp.einsum(
        "hgqk,khc->qhgc", layer_weights, value_rows, preferred_element_type=jnp.float32
    )
    return attended.astype(jnp.bfloat16)


def local(
    stream_in,
    attn_gain,
    w_qkv,
    key_value_cache,
    w_out,
    mlp_gain,
    expert_index,
    gate_weight,
    w_gateup,
    w_down,
):
    seq_count = lax.axis_size("seq")
    tp_count = lax.axis_size("tp")
    length_local = stream_in.shape[0]
    heads_local = w_qkv.shape[1]
    query_group_width = QUERY_HEADS // KEY_VALUE_HEADS
    normed = rms_scale(stream_in.astype(jnp.float32), attn_gain).astype(jnp.bfloat16)
    projected_rows = jnp.einsum(
        "td,dhc->thc", normed, w_qkv, preferred_element_type=jnp.float32
    ).astype(jnp.bfloat16)
    projected_rows = projected_rows.reshape(
        length_local, heads_local, query_group_width + 2, HEAD_SIZE
    )
    queries = projected_rows[:, :, :query_group_width]
    kv_tail_rows = jnp.concatenate(
        [
            projected_rows[length_local - WINDOW_KEYS :, :, query_group_width],
            projected_rows[length_local - WINDOW_KEYS :, :, query_group_width + 1],
        ],
        axis=-1,
    )
    earlier = from_behind(kv_tail_rows, "seq", 1)
    at_start = lax.axis_index("seq") == 0
    earlier = jnp.where(at_start, key_value_cache, earlier)
    key_rows = jnp.concatenate(
        [earlier[:, :, :HEAD_SIZE], projected_rows[:, :, query_group_width]], axis=0
    )
    value_rows = jnp.concatenate(
        [earlier[:, :, HEAD_SIZE:], projected_rows[:, :, query_group_width + 1]], axis=0
    )
    attended = window_block(queries, key_rows, value_rows).reshape(
        length_local, heads_local * query_group_width * HEAD_SIZE
    )
    block_rows = length_local // tp_count
    attn_out = lax.psum_scatter(
        jnp.dot(attended, w_out, preferred_element_type=jnp.float32).astype(jnp.bfloat16),
        "tp",
        scatter_dimension=0,
        tiled=True,
    ).astype(jnp.float32)
    own_start = lax.axis_index("tp") * block_rows
    residual = (
        lax.dynamic_slice_in_dim(stream_in, own_start, block_rows, 0).astype(jnp.float32) + attn_out
    )
    hidden_in = rms_scale(residual, mlp_gain).astype(jnp.bfloat16)
    experts_dev = w_gateup.shape[0]
    capacity = 2 * length_local * TOPK // (tp_count * EXPERTS)
    slots_dev = experts_dev * capacity
    onehot = (
        expert_index.reshape(-1)[:, None] == jnp.arange(EXPERTS, dtype=jnp.int32)[None, :]
    ).astype(jnp.int32)
    slot_rank = jnp.sum((jnp.cumsum(onehot, axis=0) - 1) * onehot, axis=1)
    slot_id = (expert_index.reshape(-1) * capacity + slot_rank).reshape(block_rows, TOPK)
    slot_grid = jnp.arange(EXPERTS * capacity, dtype=jnp.int32)
    matches = slot_grid[None, None, :] == slot_id[:, :, None]
    placer = jnp.sum(matches.astype(jnp.float32), axis=1).T.astype(jnp.bfloat16)
    packed = jnp.dot(placer, hidden_in, preferred_element_type=jnp.float32).astype(jnp.bfloat16)
    packed = packed.reshape(seq_count, slots_dev, MODEL_WIDTH)
    copies = jnp.broadcast_to(packed[:, None], (seq_count, tp_count, slots_dev, MODEL_WIDTH))
    copies = copies.reshape(seq_count * tp_count, slots_dev, MODEL_WIDTH)
    gathered = lax.all_to_all(copies, ("seq", "tp"), split_axis=0, concat_axis=0, tiled=True)
    gathered = gathered.reshape(seq_count, tp_count, experts_dev, capacity, MODEL_WIDTH)

    def one_expert(chosen, gate_up_matrix, down_proj):
        input_rows = chosen.reshape(-1, MODEL_WIDTH)
        gate_up_rows = jnp.einsum(
            "vi,ipk->vpk", input_rows, gate_up_matrix, preferred_element_type=jnp.float32
        )
        activated = (jax.nn.silu(gate_up_rows[:, 0]) * gate_up_rows[:, 1]).astype(jnp.bfloat16)
        result = jnp.dot(activated, down_proj, preferred_element_type=jnp.float32)
        return result.reshape(seq_count, tp_count, capacity, MODEL_WIDTH)

    partials = jnp.stack(
        [
            one_expert(gathered[:, :, expert], w_gateup[expert], w_down[expert])
            for expert in range(experts_dev)
        ],
        axis=2,
    )
    rounded = partials.astype(jnp.bfloat16).reshape(seq_count * tp_count, slots_dev, MODEL_WIDTH)
    returned = lax.all_to_all(rounded, ("seq", "tp"), split_axis=0, concat_axis=0, tiled=True)
    returned = returned.reshape(seq_count, tp_count, slots_dev, MODEL_WIDTH)
    returned_rows = jnp.sum(returned.astype(jnp.float32), axis=1).astype(jnp.bfloat16)
    returned_rows = returned_rows.reshape(EXPERTS * capacity, MODEL_WIDTH)
    picker = jnp.sum(gate_weight[:, :, None] * matches.astype(jnp.float32), axis=1)
    mixture = jnp.dot(picker, returned_rows.astype(jnp.float32), precision=lax.Precision.HIGHEST)
    return (residual + mixture).astype(jnp.bfloat16)


def solution(mesh):
    in_specs = (
        P("seq", None),
        P(),
        P(None, "tp", None),
        P(None, "tp", None),
        P("tp", None),
        P(),
        P(("seq", "tp"), None),
        P(("seq", "tp"), None),
        P("seq", None, None, "tp"),
        P("seq", "tp", None),
    )
    out_specs = P(("seq", "tp"), None)
    return jax.shard_map(local, mesh=mesh, in_specs=in_specs, out_specs=out_specs, check_vma=False)
```

profile of v0, /device:TPU:0, one launch (start us, length us, event | category | flops | bytes accessed | tf_op | source)
XLA Modules:
  0.0 389.3 jit_solution(5643908478327588852)
XLA Ops:
  6.5 1.5 fusion.53
  8.1 4.8 %fusion.56 = bf16[128,2,640]{2,0,1:T(8,128)(2,1)S(1)} fusion(bf16[2880,2,640]{2,1,0:T(2,128)(2,1)} %param.12, bf16[128,2880]{0,1:T(8,128)(2,1)} %param.10, f32[2880]{0:T(1024)} %param.11, f32[128]{0:T(128)S(1)} %add_rsqrt_fusion.1), kind=kOutput, calls=%fused_computation.50 | convolution fusion | flops 945356800 | bytes 8449792 | tf_op jit(solution)/shard_map/td,dhc->thc/dot_general | solution.py:63
  13.1 4.9 %collective-permute-start = (bf16[128,2,128]{0,2,1:T(8,128)(2,1)S(1)}, bf16[128,2,128]{0,2,1:T(8,128)(2,1)S(1)}, u32[]{:S(2)}, u32[]{:S(2)}) collective-permute-start(bf16[128,2,128]{0,2,1:T(8,128)(2,1)S(1)} %pad_maximum_fusion.1), channel_id=1, source_target_pairs={{0,4},{4,8},{8,12},{12,16},{16,20},{20,24},{24,28},{1,5},{5,9},{9,... | collective-permute-start | bytes 196616 | tf_op jit(solution)/shard_map/ppermute | solution.py:21
  18.2 1.7 collective-permute-done
  21.0 5.8 %convolution_convert_fusion.1 = bf16[128,2880]{1,0:T(8,128)(2,1)} fusion(bf16[128,1024]{0,1:T(8,128)(2,1)S(1)} %bitcast.153, bf16[1024,2880]{0,1:T(8,128)(2,1)} %param.14), kind=kOutput, calls=%fused_computation.38 | convolution fusion | flops 755343360 | bytes 6897664 | tf_op jit(solution)/shard_map/dot_general | solution.py:91
  28.4 23.8 %reduce-scatter.2.cloned.1.call-done = bf16[32,2880]{1,0:T(8,128)(2,1)} async-done(((bf16[128,2880]{1,0:T(8,128)(2,1)}), bf16[32,2880]{1,0:T(8,128)(2,1)}) %reduce-scatter.2.cloned.1.call-update) | async-done | bytes 184336 | tf_op jit(solution)/shard_map/reduce_scatter | solution.py:90
  52.1 1.1 multiply_reduce_fusion
  53.3 1.6 convolution_convert_fusion
  54.9 1.0 copy.78
  56.3 137.4 %all_to_all.10 = bf16[32,32,2880]{2,1,0:T(8,128)(2,1)S(1)} all-to-all(bf16[32,32,2880]{2,1,0:T(8,128)(2,1)S(1)} %bitcast.139), channel_id=1, replica_groups=mesh['seq'=8,'tp'=4] {'seq','tp'}, dimensions={0} | all-to-all | bytes 11796480 | tf_op jit(solution)/shard_map/all_to_all | solution.py:116
  193.7 1.7 fusion.93
  195.4 5.9 %fusion.7 = f32[256,2,720]{0,2,1:T(8,128)S(1)} fusion(bf16[256,2880,1]{1,0,2:T(8,128)(2,1)S(1)} %bitcast.146, bf16[4,2880,2,720]{1,3,2,0:T(8,128)(2,1)} %param.18), kind=kOutput, calls=%fused_computation.7 | convolution fusion | flops 2123366400 | bytes 11427840 | tf_op jit(solution)/shard_map/vi,ipk->vpk/dot_general | solution.py:121
  201.5 5.9 %fusion.1 = f32[256,2,720]{0,2,1:T(8,128)S(1)} fusion(bf16[256,2880,1]{1,0,2:T(8,128)(2,1)S(1)} %bitcast.145, bf16[4,2880,2,720]{1,3,2,0:T(8,128)(2,1)} %param.18), kind=kOutput, calls=%fused_computation.1 | convolution fusion | flops 2123366400 | bytes 11427840 | tf_op jit(solution)/shard_map/vi,ipk->vpk/dot_general | solution.py:121
  209.5 3.8 fusion.48
  213.3 4.9 %fusion.39 = bf16[8,4,1,8,2880]{4,3,1,0,2:T(8,128)(2,1)} fusion(bf16[8,4,8,720]{3,2,1,0:T(8,128)(2,1)S(1)} %bitcast.149, bf16[4,720,2880]{2,1,0:T(8,128)(2,1)} %param.19), kind=kOutput, calls=%fused_computation.34 | convolution fusion | flops 1062420480 | bytes 6082560 | tf_op jit(solution)/shard_map/dot_general | solution.py:125
  218.1 5.9 %fusion.3 = f32[256,2,720]{0,2,1:T(8,128)S(1)} fusion(bf16[256,2880,1]{1,0,2:T(8,128)(2,1)S(1)} %bitcast.144, bf16[4,2880,2,720]{1,3,2,0:T(8,128)(2,1)} %param.18), kind=kOutput, calls=%fused_computation.3 | convolution fusion | flops 2123366400 | bytes 11427840 | tf_op jit(solution)/shard_map/vi,ipk->vpk/dot_general | solution.py:121
  224.0 1.0 fusion.65
  225.0 5.9 %fusion.5 = f32[256,2,720]{0,2,1:T(8,128)S(1)} fusion(bf16[256,2880,1]{1,0,2:T(8,128)(2,1)S(1)} %bitcast.143, bf16[4,2880,2,720]{1,3,2,0:T(8,128)(2,1)} %param.18), kind=kOutput, calls=%fused_computation.5 | convolution fusion | flops 2123366400 | bytes 11427840 | tf_op jit(solution)/shard_map/vi,ipk->vpk/dot_general | solution.py:121
  232.0 0.9 copy.84
  233.0 4.0 %fusion.42 = bf16[8,4,1,8,2880]{4,3,1,0,2:T(8,128)(2,1)S(1)} fusion(bf16[8,4,8,720]{3,2,1,0:T(8,128)(2,1)} %bitcast.152, bf16[4,720,2880]{2,1,0:T(8,128)(2,1)} %param.19), kind=kOutput, calls=%fused_computation.35 | convolution fusion | flops 1062420480 | bytes 6107136 | tf_op jit(solution)/shard_map/dot_general | solution.py:125
  237.0 3.7 fusion.45
  240.7 2.2 pad_maximum_fusion
  243.6 136.5 %all_to_all.11 = bf16[32,32,2880]{2,1,0:T(8,128)(2,1)S(1)} all-to-all(bf16[32,32,2880]{2,1,0:T(8,128)(2,1)S(1)} %bitcast.140), channel_id=1, replica_groups=mesh['seq'=8,'tp'=4] {'seq','tp'}, dimensions={0} | all-to-all | bytes 11796480 | tf_op jit(solution)/shard_map/all_to_all | solution.py:136
  381.0 1.5 fusion.51
  (55 shorter events, 8.4 us)
Async XLA Ops:
  6.5 45.6 %reduce-scatter.2.cloned.1.call-start = ((), (), s32[]{:S(2)}) async-start(), calls=%async_computation.3 | async-start | bytes 942080 | tf_op jit(solution)/shard_map/reduce_scatter | solution.py:90
  8.1 9.9 %copy-start.7 = (bf16[128,2,128]{2,1,0:T(2,128)(2,1)S(1)}, bf16[128,2,128]{2,1,0:T(2,128)(2,1)}, u32[]{:S(2)}) copy-start(bf16[128,2,128]{2,1,0:T(2,128)(2,1)} %param.13) | copy-start | bytes 196612
  13.1 6.8 %collective-permute-start = (bf16[128,2,128]{0,2,1:T(8,128)(2,1)S(1)}, bf16[128,2,128]{0,2,1:T(8,128)(2,1)S(1)}, u32[]{:S(2)}, u32[]{:S(2)}) collective-permute-start(bf16[128,2,128]{0,2,1:T(8,128)(2,1)S(1)} %pad_maximum_fusion.1), channel_id=1, source_target_pairs={{0,4},{4,8},{8,12},{12,16},{16,20},{20,24},{24,28},{1,5},{5,9},{9,... | collective-permute-start | bytes 196616 | tf_op jit(solution)/shard_map/ppermute | solution.py:21
  21.0 5.8 %copy-start.9 = (s32[32,4]{0,1:T(4,128)S(1)}, s32[32,4]{0,1:T(4,128)}, u32[]{:S(2)}) copy-start(s32[32,4]{0,1:T(4,128)} %param.16) | copy-start | bytes 1540
  21.0 6.7 %copy-start = (bf16[128,2880]{0,1:T(8,128)(2,1)S(1)}, bf16[128,2880]{0,1:T(8,128)(2,1)}, u32[]{:S(2)}) copy-start(bf16[128,2880]{0,1:T(8,128)(2,1)} %param.10) | copy-start | bytes 2211844
  26.8 1.4 copy-start.10
  26.8 26.4 %copy-start.8 = (f32[2880]{0:T(1024)S(1)}, f32[2880]{0:T(1024)}, u32[]{:S(2)}) copy-start(f32[2880]{0:T(1024)} %param.15) | copy-start | bytes 34564
  209.5 3.8 copy-start.5
  213.2 4.9 %copy-start.2 = (bf16[8,4,1,8,2880]{4,3,2,1,0:T(8,128)(2,1)S(1)}, bf16[8,4,1,8,2880]{4,3,2,1,0:T(8,128)(2,1)}, u32[]{:S(2)}) copy-start(bf16[8,4,1,8,2880]{4,3,2,1,0:T(8,128)(2,1)} %get-tuple-element.9) | copy-start | bytes 4423684
  230.9 1.2 copy-start.4
  233.0 4.0 %copy-start.6 = (bf16[256,1,720]{2,0,1:T(8,128)(2,1)S(1)}, bf16[256,1,720]{2,0,1:T(8,128)(2,1)}, u32[]{:S(2)}) copy-start(bf16[256,1,720]{2,0,1:T(8,128)(2,1)} %copy.82) | copy-start | bytes 1105924
  237.0 3.7 copy-start.3
  380.1 0.9 copy-start.1
Sparse Core Ops, SparseCore 0:
  27.0 25.1 reduce-scatter.1
where the time goes:
time: 390 us; the launch traced here: 389 us
  blocking collectives  274 us (70%)
  matrix products  54.6 us (14%)
  waiting for transfers between devices  25.5 us (7%)
  between operations  13.8 us (4%)
  local copies, waits for them, and re-layouts  8.8 us (2%)
  other arithmetic  7.88 us (2%)
  starting transfers between devices  4.88 us (1%)
    all_to_all x1, blocking collectives, local(): lax.all_to_all(copies, ('seq', 'tp'), split_axis=0, concat_axis=0, tiled=...  137 us
    all_to_all x1, blocking collectives, local(): lax.all_to_all(rounded, ('seq', 'tp'), split_axis=0, concat_axis=0, tiled...  137 us
    reduce_scatter x1, waiting for transfers between devices, local(): lax.psum_scatter(jnp.dot(attended, w_out, preferred_element_type=jnp.floa...  23.8 us
    dot_general x4, matrix products, one_expert(): jnp.einsum('vi,ipk->vpk', input_rows, gate_up_matrix, preferred_element_t...  23.6 us
    dot_general x4, matrix products, one_expert(): result = jnp.dot(activated, down_proj, preferred_element_type=jnp.float32)  16.3 us
  transfers between devices with their start and end apart: 2, of which 2 were waited for; matrix products, arithmetic and copies ran while one was open for 0% of the time, Pallas kernels for 0%

commit v1 on v0

--- a/solution.py
+++ b/solution.py
@@ -100,46 +100,53 @@
     hidden_in = rms_scale(residual, mlp_gain).astype(jnp.bfloat16)
     experts_dev = w_gateup.shape[0]
     capacity = 2 * length_local * TOPK // (tp_count * EXPERTS)
-    slots_dev = experts_dev * capacity
-    onehot = (
-        expert_index.reshape(-1)[:, None] == jnp.arange(EXPERTS, dtype=jnp.int32)[None, :]
-    ).astype(jnp.int32)
-    slot_rank = jnp.sum((jnp.cumsum(onehot, axis=0) - 1) * onehot, axis=1)
-    slot_id = (expert_index.reshape(-1) * capacity + slot_rank).reshape(block_rows, TOPK)
-    slot_grid = jnp.arange(EXPERTS * capacity, dtype=jnp.int32)
-    matches = slot_grid[None, None, :] == slot_id[:, :, None]
-    placer = jnp.sum(matches.astype(jnp.float32), axis=1).T.astype(jnp.bfloat16)
-    packed = jnp.dot(placer, hidden_in, preferred_element_type=jnp.float32).astype(jnp.bfloat16)
-    packed = packed.reshape(seq_count, slots_dev, MODEL_WIDTH)
-    copies = jnp.broadcast_to(packed[:, None], (seq_count, tp_count, slots_dev, MODEL_WIDTH))
-    copies = copies.reshape(seq_count * tp_count, slots_dev, MODEL_WIDTH)
-    gathered = lax.all_to_all(copies, ("seq", "tp"), split_axis=0, concat_axis=0, tiled=True)
-    gathered = gathered.reshape(seq_count, tp_count, experts_dev, capacity, MODEL_WIDTH)
+    blocks = seq_count * tp_count
+    group_blocks = max(1, min(blocks, 256 // block_rows))
+    groups = blocks // group_blocks
+    tokens_all = blocks * block_rows
 
-    def one_expert(chosen, gate_up_matrix, down_proj):
-        input_rows = chosen.reshape(-1, MODEL_WIDTH)
+    index_all = lax.all_gather(expert_index, ("seq", "tp"), axis=0, tiled=True)
+    gate_all = lax.all_gather(gate_weight, ("seq", "tp"), axis=0, tiled=True)
+    own_experts = lax.axis_index("seq") * experts_dev + jnp.arange(experts_dev, dtype=jnp.int32)
+    named = index_all[:, :, None] == own_experts[None, None, :]
+    member = jnp.any(named, axis=1).reshape(blocks, block_rows, experts_dev)
+    gate_token = jnp.sum(jnp.where(named, gate_all[:, :, None], 0.0), axis=1)
+    gate_token = gate_token.reshape(blocks, block_rows, experts_dev)
+    rank = jnp.cumsum(member.astype(jnp.int32), axis=1) - 1
+    slot = jnp.where(member, rank, -1)
+    hot = slot[:, :, :, None] == jnp.arange(capacity, dtype=jnp.int32)
+    gate_slot = jnp.sum(hot * gate_token[:, :, :, None], axis=1)
+    gate_slot = jnp.moveaxis(gate_slot, 1, 0).reshape(experts_dev, blocks * capacity)
+    hot = hot.reshape(groups, group_blocks, block_rows, experts_dev, capacity)
+    same = jnp.eye(group_blocks, dtype=jnp.bool_)
+    wide = hot[:, :, :, :, None, :] & same[None, :, None, None, :, None]
+    placer = wide.reshape(
+        groups, group_blocks * block_rows, experts_dev * group_blocks * capacity
+    ).astype(jnp.bfloat16)
+
+    tokens = lax.all_gather(hidden_in, ("seq", "tp"), axis=0, tiled=True)
+    tokens = tokens.reshape(groups, group_blocks * block_rows, MODEL_WIDTH)
+    packed = jnp.einsum("gts,gtd->gsd", placer, tokens, preferred_element_type=jnp.float32)
+    packed = packed.astype(jnp.bfloat16).reshape(
+        groups, experts_dev, group_blocks * capacity, MODEL_WIDTH
+    )
+
+    def one_expert(expert):
+        input_rows = packed[:, expert].reshape(-1, MODEL_WIDTH)
         gate_up_rows = jnp.einsum(
-            "vi,ipk->vpk", input_rows, gate_up_matrix, preferred_element_type=jnp.float32
+            "vi,ipk->vpk", input_rows, w_gateup[expert], preferred_element_type=jnp.float32
         )
-        activated = (jax.nn.silu(gate_up_rows[:, 0]) * gate_up_rows[:, 1]).astype(jnp.bfloat16)
-        result = jnp.dot(activated, down_proj, preferred_element_type=jnp.float32)
-        return result.reshape(seq_count, tp_count, capacity, MODEL_WIDTH)
+        activated = jax.nn.silu(gate_up_rows[:, 0]) * gate_up_rows[:, 1]
+        activated = (activated * gate_slot[expert][:, None]).astype(jnp.bfloat16)
+        result = jnp.dot(activated, w_down[expert], preferred_element_type=jnp.float32)
+        return result.astype(jnp.bfloat16).reshape(groups, group_blocks * capacity, MODEL_WIDTH)
 
-    partials = jnp.stack(
-        [
-            one_expert(gathered[:, :, expert], w_gateup[expert], w_down[expert])
-            for expert in range(experts_dev)
-        ],
-        axis=2,
-    )
-    rounded = partials.astype(jnp.bfloat16).reshape(seq_count * tp_count, slots_dev, MODEL_WIDTH)
-    returned = lax.all_to_all(rounded, ("seq", "tp"), split_axis=0, concat_axis=0, tiled=True)
-    returned = returned.reshape(seq_count, tp_count, slots_dev, MODEL_WIDTH)
-    returned_rows = jnp.sum(returned.astype(jnp.float32), axis=1).astype(jnp.bfloat16)
-    returned_rows = returned_rows.reshape(EXPERTS * capacity, MODEL_WIDTH)
-    picker = jnp.sum(gate_weight[:, :, None] * matches.astype(jnp.float32), axis=1)
-    mixture = jnp.dot(picker, returned_rows.astype(jnp.float32), precision=lax.Precision.HIGHEST)
-    return (residual + mixture).astype(jnp.bfloat16)
+    results = jnp.stack([one_expert(expert) for expert in range(experts_dev)], axis=1)
+    results = results.reshape(groups, experts_dev * group_blocks * capacity, MODEL_WIDTH)
+    summed = jnp.einsum("gts,gsd->gtd", placer, results, preferred_element_type=jnp.float32)
+    summed = summed.astype(jnp.bfloat16).reshape(tokens_all, MODEL_WIDTH)
+    mixture = lax.psum_scatter(summed, ("seq", "tp"), scatter_dimension=0, tiled=True)
+    return (residual + mixture.astype(jnp.float32)).astype(jnp.bfloat16)
 
 
 def solution(mesh):

time: 390 us -> 391 us (level)
  blocking collectives: 274 us -> 78.3 us
  waiting for transfers between devices: 25.5 us -> 169 us
  local copies, waits for them, and re-layouts: 8.8 us -> 40.4 us
  matrix products: 54.6 us -> 71.4 us
  other arithmetic: 7.88 us -> 12.9 us
    all_to_all x2 -> x0, blocking collectives: 274 us -> none  [the longest x1 137 us: local(): lax.all_to_all(copies, ('seq', 'tp'), split_axis=0, concat_axis=0, tiled=...]
    reduce_scatter x0 -> x1, waiting for transfers between devices: none -> 142 us  [local(): lax.psum_scatter(summed, ('seq', 'tp'), scatter_dimension=0, tiled=True)]
    all_gather x0 -> x2, blocking collectives: none -> 78.3 us  [the longest x1 41.2 us: local(): index_all = lax.all_gather(expert_index, ('seq', 'tp'), axis=0, tiled=True)]
    convert_element_type x5 -> x8, local copies, waits for them, and re-layouts: 4.66 us -> 28.1 us  [the longest x1 8.47 us: local(): summed = summed.astype(jnp.bfloat16).reshape(tokens_all, MODEL_WIDTH)]
    dot_general x10, matrix products: 43 us -> 59.8 us  [the longest x4 26.4 us: one_expert(): jnp.einsum('vi,ipk->vpk', input_rows, w_gateup[expert], preferred_element...]
  transfers between devices with their start and end apart: 2 -> 4, of which waited for: 2 -> 3; matrix products, arithmetic and copies ran while one was open for 0% -> 3% of each run, Pallas kernels for 0% -> 0%
where the time goes in v1:
time: 391 us; the launch traced here: 390 us
  waiting for transfers between devices  169 us (43%)
  blocking collectives  78.3 us (20%)
  matrix products  71.4 us (18%)
  local copies, waits for them, and re-layouts  40.4 us (10%)
  between operations  13.4 us (3%)
  other arithmetic  12.9 us (3%)
  starting transfers between devices  4.96 us (1%)
    reduce_scatter x1, waiting for transfers between devices, local(): lax.psum_scatter(summed, ('seq', 'tp'), scatter_dimension=0, tiled=True)  142 us
    all_gather x1, blocking collectives, local(): index_all = lax.all_gather(expert_index, ('seq', 'tp'), axis=0, tiled=True)  41.2 us
    all_gather x1, blocking collectives, local(): gate_all = lax.all_gather(gate_weight, ('seq', 'tp'), axis=0, tiled=True)  37.2 us
    dot_general x4, matrix products, one_expert(): jnp.einsum('vi,ipk->vpk', input_rows, w_gateup[expert], preferred_element...  26.4 us
    reduce_scatter x1, waiting for transfers between devices, local(): lax.psum_scatter(jnp.dot(attended, w_out, preferred_element_type=jnp.floa...  24.7 us
    dot_general x4, matrix products, one_expert(): jnp.dot(activated, w_down[expert], preferred_element_type=jnp.float32)  20.7 us
    convert_element_type x1, local copies, waits for them, and re-layouts, local(): summed = summed.astype(jnp.bfloat16).reshape(tokens_all, MODEL_WIDTH)  8.47 us
    convert_element_type x1, local copies, waits for them, and re-layouts, local(): packed.astype(jnp.bfloat16)  8.47 us
  transfers between devices with their start and end apart: 4, of which 3 were waited for; matrix products, arithmetic and copies ran while one was open for 3% of the time, Pallas kernels for 0%

profile of v1, /device:TPU:0, one launch (start us, length us, event | category | flops | bytes accessed | tf_op | source)
XLA Modules:
  0.0 390.0 jit_solution(17290031250632482186)
XLA Ops:
  8.1 4.8 %fusion.43 = bf16[128,2,640]{2,0,1:T(8,128)(2,1)S(1)} fusion(bf16[2880,2,640]{2,1,0:T(2,128)(2,1)} %param.12, bf16[128,2880]{0,1:T(8,128)(2,1)} %param.10, f32[2880]{0:T(1024)} %param.11, f32[128]{0:T(128)S(1)} %add_rsqrt_fusion.1), kind=kOutput, calls=%fused_computation.44 | convolution fusion | flops 945356800 | bytes 8449792 | tf_op jit(solution)/shard_map/td,dhc->thc/dot_general | solution.py:63
  13.1 4.9 %collective-permute-start = (bf16[128,2,128]{0,2,1:T(8,128)(2,1)S(1)}, bf16[128,2,128]{0,2,1:T(8,128)(2,1)S(1)}, u32[]{:S(2)}, u32[]{:S(2)}) collective-permute-start(bf16[128,2,128]{0,2,1:T(8,128)(2,1)S(1)} %pad_maximum_fusion.1), channel_id=1, source_target_pairs={{0,4},{4,8},{8,12},{12,16},{16,20},{20,24},{24,28},{1,5},{5,9},{9,... | collective-permute-start | bytes 196616 | tf_op jit(solution)/shard_map/ppermute | solution.py:21
  21.0 5.8 %convolution_convert_fusion.2 = bf16[128,2880]{1,0:T(8,128)(2,1)} fusion(bf16[128,1024]{0,1:T(8,128)(2,1)S(1)} %bitcast.155, bf16[1024,2880]{0,1:T(8,128)(2,1)} %param.14), kind=kOutput, calls=%fused_computation.34 | convolution fusion | flops 755343360 | bytes 6897664 | tf_op jit(solution)/shard_map/dot_general | solution.py:91
  27.4 24.7 %reduce-scatter.3.cloned.1.call-done = bf16[32,2880]{1,0:T(8,128)(2,1)} async-done(((bf16[128,2880]{1,0:T(8,128)(2,1)}), bf16[32,2880]{1,0:T(8,128)(2,1)}) %reduce-scatter.3.cloned.1.call-update) | async-done | bytes 184336 | tf_op jit(solution)/shard_map/reduce_scatter | solution.py:90
  55.0 41.2 %all-gather = s32[32,32,4]{1,2,0:T(4,128)S(1)} all-gather(s32[1,32,4]{1,2,0:T(4,128)S(1)} %bitcast.156), channel_id=1, replica_groups=mesh['seq'=8,'tp'=4] {'seq','tp'}, dimensions={0}, use_global_device_ids=true | all-gather | bytes 16896 | tf_op jit(solution)/shard_map/all_gather | solution.py:108
  96.7 2.9 copy.97
  104.4 37.2 %all-gather.1 = f32[32,32,4]{1,2,0:T(4,128)S(1)} all-gather(f32[1,32,4]{1,2,0:T(4,128)S(1)} %bitcast.157), channel_id=1, replica_groups=mesh['seq'=8,'tp'=4] {'seq','tp'}, dimensions={0}, use_global_device_ids=true | all-gather | bytes 16896 | tf_op jit(solution)/shard_map/all_gather | solution.py:109
  145.5 7.6 %convolution_convert_fusion.1 = bf16[4,256,2880]{1,2,0:T(8,128)(2,1)} fusion(bf16[4,256,2880]{2,1,0:T(8,128)(2,1)} %bitcast.143, pred[4,256,256]{1,2,0:T(32,128)(4,1)S(1)} %and.27, pred[256,256]{0,1:T(8,128)(4,1)S(1)} %and.29), kind=kOutput, calls=%fused_computation.17 | convolution fusion | flops 1513160704 | bytes 12124160 | tf_op jit(solution)/shard_map/gts,gtd->gsd/dot_general | solution.py:129
  153.1 8.5 %copy.102 = bf16[4,256,2880]{2,1,0:T(8,128)(2,1)} copy(bf16[4,256,2880]{1,2,0:T(8,128)(2,1)} %convolution_convert_fusion.1) | data formatting | bytes 11796480 | tf_op jit(solution)/shard_map/convert_element_type | solution.py:130
  161.5 5.0 %fusion.101 = (bf16[4,1,64,2880]{3,2,1,0:T(8,128)(2,1)S(1)}, bf16[4,1,64,2880]{3,2,1,0:T(8,128)(2,1)S(1)}, bf16[4,1,64,2880]{3,2,1,0:T(8,128)(2,1)}, bf16[4,1,64,2880]{3,2,1,0:T(8,128)(2,1)}) fusion(bf16[4,4,64,2880]{3,2,1,0:T(8,128)(2,1)} %bitcast.141), kind=kLoop, calls=%fused_computation.121 | loop fusion | bytes 11796480 | tf_op jit(solution)/shard_map/slice | solution.py:135
  166.5 7.0 %fusion.7 = f32[256,2,720]{0,2,1:T(8,128)} fusion(bf16[256,2880,1]{1,0,2:T(8,128)(2,1)S(1)} %bitcast.151, bf16[4,2880,2,720]{1,3,2,0:T(8,128)(2,1)} %param.18), kind=kOutput, calls=%fused_computation.7 | convolution fusion | flops 2123366400 | bytes 11427840 | tf_op jit(solution)/shard_map/vi,ipk->vpk/dot_general | solution.py:136
  173.6 5.9 %fusion.1 = f32[256,2,720]{0,2,1:T(8,128)S(1)} fusion(bf16[256,2880,1]{1,0,2:T(8,128)(2,1)S(1)} %bitcast.150, bf16[4,2880,2,720]{1,3,2,0:T(8,128)(2,1)} %param.18), kind=kOutput, calls=%fused_computation.1 | convolution fusion | flops 2123366400 | bytes 11427840 | tf_op jit(solution)/shard_map/vi,ipk->vpk/dot_general | solution.py:136
  179.5 4.1 %fusion.36 = bf16[256,2880]{0,1:T(8,128)(2,1)S(1)} fusion(bf16[4,720,2880]{2,1,0:T(8,128)(2,1)} %param.19, f32[256,2,720]{0,2,1:T(8,128)S(1)} %fusion.1, f32[256]{0:T(256)S(1)} %mul.175), kind=kOutput, calls=%fused_computation.33 | convolution fusion | flops 1063710720 | bytes 7189504 | tf_op jit(solution)/shard_map/dot_general | solution.py:141
  184.6 5.7 %fusion.27 = bf16[256,2880]{0,1:T(8,128)(2,1)} fusion(bf16[4,720,2880]{2,1,0:T(8,128)(2,1)} %param.19, f32[256,2,720]{0,2,1:T(8,128)} %fusion.7, f32[256]{0:T(256)S(1)} %mul.160), kind=kOutput, calls=%fused_computation.30 | convolution fusion | flops 1063710720 | bytes 7189504 | tf_op jit(solution)/shard_map/dot_general | solution.py:141
  192.3 6.5 %fusion.3 = f32[256,2,720]{0,2,1:T(8,128)S(1)} fusion(bf16[256,2880,1]{1,0,2:T(8,128)(2,1)} %bitcast.149, bf16[4,2880,2,720]{1,3,2,0:T(8,128)(2,1)} %param.18), kind=kOutput, calls=%fused_computation.3 | convolution fusion | flops 2123366400 | bytes 11460608 | tf_op jit(solution)/shard_map/vi,ipk->vpk/dot_general | solution.py:136
  198.8 7.0 %fusion.5 = f32[256,2,720]{0,2,1:T(8,128)} fusion(bf16[256,2880,1]{1,0,2:T(8,128)(2,1)S(1)} %bitcast.148, bf16[4,2880,2,720]{1,3,2,0:T(8,128)(2,1)} %param.18), kind=kOutput, calls=%fused_computation.5 | convolution fusion | flops 2123366400 | bytes 11427840 | tf_op jit(solution)/shard_map/vi,ipk->vpk/dot_general | solution.py:136
  205.8 5.2 %fusion.33 = bf16[256,2880]{0,1:T(8,128)(2,1)} fusion(bf16[4,720,2880]{2,1,0:T(8,128)(2,1)} %param.19, f32[256,2,720]{0,2,1:T(8,128)S(1)} %fusion.3, f32[256]{0:T(256)S(1)} %mul.170), kind=kOutput, calls=%fused_computation.32 | convolution fusion | flops 1063710720 | bytes 7189504 | tf_op jit(solution)/shard_map/dot_general | solution.py:141
  211.0 2.6 copy.112
  213.6 5.7 %fusion.30 = bf16[256,2880]{0,1:T(8,128)(2,1)} fusion(bf16[4,720,2880]{2,1,0:T(8,128)(2,1)} %param.19, f32[256,2,720]{0,2,1:T(8,128)} %fusion.5, f32[256]{0:T(256)S(1)} %mul.165), kind=kOutput, calls=%fused_computation.31 | convolution fusion | flops 1063710720 | bytes 7189504 | tf_op jit(solution)/shard_map/dot_general | solution.py:141
  219.3 2.5 copy.110
  221.8 3.8 pad_maximum_fusion
  226.2 5.0 %convolution_convert_fusion = bf16[4,256,2880]{1,2,0:T(8,128)(2,1)} fusion(bf16[4,256,2880]{2,1,0:T(8,128)(2,1)S(1)} %bitcast.142, pred[4,256,256]{1,2,0:T(32,128)(4,1)S(1)} %and.27, pred[256,256]{0,1:T(8,128)(4,1)S(1)} %and.29), kind=kOutput, calls=%fused_computation.16 | convolution fusion | flops 1513160704 | bytes 12124160 | tf_op jit(solution)/shard_map/gts,gsd->gtd/dot_general | solution.py:146
  231.3 8.5 %copy.118 = bf16[4,256,2880]{2,1,0:T(8,128)(2,1)} copy(bf16[4,256,2880]{1,2,0:T(8,128)(2,1)} %convolution_convert_fusion) | data formatting | bytes 11796480 | tf_op jit(solution)/shard_map/convert_element_type | solution.py:147
  239.7 142.1 %reduce-scatter.5.cloned.1.call-done = bf16[32,2880]{1,0:T(8,128)(2,1)} async-done(((bf16[1024,2880]{1,0:T(8,128)(2,1)}), bf16[32,2880]{1,0:T(8,128)(2,1)}) %reduce-scatter.5.cloned.1.call-update) | async-done | bytes 184336 | tf_op jit(solution)/shard_map/reduce_scatter | solution.py:148
  (72 shorter events, 22.5 us)
Async XLA Ops:
  6.5 45.6 %reduce-scatter.3.cloned.1.call-start = ((), (), s32[]{:S(2)}) async-start(), calls=%async_computation.2 | async-start | bytes 942080 | tf_op jit(solution)/shard_map/reduce_scatter | solution.py:90
  8.1 9.9 %copy-start.3 = (bf16[128,2,128]{2,1,0:T(2,128)(2,1)S(1)}, bf16[128,2,128]{2,1,0:T(2,128)(2,1)}, u32[]{:S(2)}) copy-start(bf16[128,2,128]{2,1,0:T(2,128)(2,1)} %param.13) | copy-start | bytes 196612
  13.1 6.8 %collective-permute-start = (bf16[128,2,128]{0,2,1:T(8,128)(2,1)S(1)}, bf16[128,2,128]{0,2,1:T(8,128)(2,1)S(1)}, u32[]{:S(2)}, u32[]{:S(2)}) collective-permute-start(bf16[128,2,128]{0,2,1:T(8,128)(2,1)S(1)} %pad_maximum_fusion.1), channel_id=1, source_target_pairs={{0,4},{4,8},{8,12},{12,16},{16,20},{20,24},{24,28},{1,5},{5,9},{9,... | collective-permute-start | bytes 196616 | tf_op jit(solution)/shard_map/ppermute | solution.py:21
  21.0 5.9 %copy-start = (bf16[128,2880]{0,1:T(8,128)(2,1)S(1)}, bf16[128,2880]{0,1:T(8,128)(2,1)}, u32[]{:S(2)}) copy-start(bf16[128,2880]{0,1:T(8,128)(2,1)} %param.10) | copy-start | bytes 2211844
  26.8 26.4 %copy-start.4 = (f32[2880]{0:T(1024)S(1)}, f32[2880]{0:T(1024)}, u32[]{:S(2)}) copy-start(f32[2880]{0:T(1024)} %param.15) | copy-start | bytes 34564
  26.8 28.2 %copy-start.5 = (s32[32,4]{0,1:T(4,128)S(1)}, s32[32,4]{0,1:T(4,128)}, u32[]{:S(2)}) copy-start(s32[32,4]{0,1:T(4,128)} %param.16) | copy-start | bytes 1540
  26.8 118.6 %all-gather.4.cloned.1.call-start = ((), (), s32[]{:S(2)}) async-start(), calls=%async_computation.3 | async-start | bytes 6217728 | tf_op jit(solution)/shard_map/all_gather | solution.py:127
  55.0 326.8 %reduce-scatter.5.cloned.1.call-start = ((), (), s32[]{:S(2)}) async-start(), calls=%async_computation.4 | async-start | bytes 6217728 | tf_op jit(solution)/shard_map/reduce_scatter | solution.py:148
  102.1 2.3 copy-start.6
  192.3 6.5 %copy-start.2 = (bf16[4,1,64,2880]{3,2,1,0:T(8,128)(2,1)S(1)}, bf16[4,1,64,2880]{3,2,1,0:T(8,128)(2,1)}, u32[]{:S(2)}) copy-start(bf16[4,1,64,2880]{3,2,1,0:T(8,128)(2,1)} %get-tuple-element.12) | copy-start | bytes 4423684
  239.7 142.1 %copy-start.1 = (bf16[32,2880]{1,0:T(8,128)(2,1)S(1)}, bf16[32,2880]{1,0:T(8,128)(2,1)}, u32[]{:S(2)}) copy-start(bf16[32,2880]{1,0:T(8,128)(2,1)} %reduce-scatter.3.cloned.1.call-done) | copy-start | bytes 552964
Sparse Core Ops, SparseCore 0:
  26.9 25.1 reduce-scatter.2
  55.4 68.8 all-gather.3
  239.9 141.8 reduce-scatter.4
